TPU v7x, 32 devices: a whole 2x2x4 slice. The times are simulated.
32 devices in a mesh: groups: 2 (over x), wide: 16 (over z, y, core).
Axes of the slice: x: 2, y: 2, z: 4, core: 2. Of those that a mesh axis runs over, the one named last changes fastest.
Arguments:
- picture_feature_maps: bfloat16 [256, 10, 10, 1536], P(('groups', 'wide')), parts along dimension 0, may hold values from -6 to 6
- partitioned_filter_tensor: bfloat16 [3, 3, 128, 1536], replicated, may hold values from -0.1875 to 0.1875
- picture_token_layer_scaling: float32 [1536], replicated, may hold values from 0.1 to 1.9
- summary_probes: bfloat16 [64, 1536], replicated, may hold values from -6 to 6
- summary_probe_layer_scaling: float32 [1536], replicated, may hold values from 0.1 to 1.9
- asking_projection_tensor: bfloat16 [1536, 1536], P('wide'), may hold values from -0.15625 to 0.15625
- lookup_projection_tensor: bfloat16 [1536, 1536], P('wide'), may hold values from -0.15625 to 0.15625
- content_projection_tensor: bfloat16 [1536, 1536], P('wide'), may hold values from -0.15625 to 0.15625
- final_projection_tensor: bfloat16 [1536, 1536], P(None, 'wide'), may hold values from -0.15625 to 0.15625
- sharpness_coefficient: float32 [16], replicated, may hold values from 0.5 to 64
Outputs:
- attended: float32 [128, 1536], P('groups'), parts along dimension 0
- new_latents: bfloat16 [128, 1536], P('groups'), parts along dimension 0
There are 2 independent parts, one for each index of `groups`. A program takes and returns all parts, laid end to end along the dimension named above; an argument that names none is the same for every part. Nothing has to cross between parts.
All inputs are finite; a program needn't handle non-finite values.
Results may differ from a plain program's by a relative error of at most 0.004.
The roundings to bfloat16 on the way count: a program that leaves them out, or rounds other values in their place, can miss the bound.
Values may be sent and summed in bfloat16 or wider, within the bound.
A program may use at most 128 MiB of HBM per device.

v0:
```python
import math

import jax
import jax.numpy as jnp
from jax import lax
from jax.sharding import PartitionSpec as P

RESIDUAL_SCALE = 0.2
EPSILON = 1e-06


def layer_norm(values, gain):
    center = values - jnp.mean(values, axis=-1, keepdims=True)
    spread = jnp.mean(center * center, axis=-1, keepdims=True)
    return center * lax.rsqrt(spread + EPSILON) * gain


def combine(left_side, right_side):
    left_max, left_sum, left_weighted = left_side
    right_max, right_sum, right_weighted = right_side
    joint_max = jnp.maximum(left_max, right_max)
    scale_left = jnp.exp(left_max - joint_max)
    scale_right = jnp.exp(right_max - joint_max)
    return (
        joint_max,
        left_sum * scale_left + right_sum * scale_right,
        left_weighted * scale_left[..., None] + right_weighted * scale_right[..., None],
    )


def merge_all(row_max, row_sum, weighted):
    joint_max = lax.pmax(row_max, "wide")
    factor = jnp.exp(row_max - joint_max)
    joint_sum, joint_weighted = lax.psum((row_sum * factor, weighted * factor[..., None]), "wide")
    return (joint_max, joint_sum, joint_weighted)


def softmax_terms(scores, carried):
    row_max = jnp.max(scores, axis=-1)
    weights = jnp.exp(scores - row_max[..., None])
    row_sum = jnp.sum(weights, axis=-1)
    weighted = jnp.einsum("hlt,thd->hld", weights, carried, precision=lax.Precision.HIGHEST)
    return (row_max, row_sum, weighted)


def per_device(
    picture_feature_maps,
    partitioned_filter_tensor,
    picture_token_layer_scaling,
    summary_probes,
    summary_probe_layer_scaling,
    asking_projection_tensor,
    lookup_projection_tensor,
    content_projection_tensor,
    final_projection_tensor,
    sharpness_coefficient,
):
    channels = picture_feature_maps.shape[3]
    subspace_number_overall = sharpness_coefficient.shape[0]
    subspace_breadth = channels // subspace_number_overall
    lat_count = summary_probes.shape[0]
    activated = jax.nn.gelu(picture_feature_maps.astype(jnp.float32)).astype(jnp.bfloat16)
    convolved = lax.conv_general_dilated(
        activated,
        partitioned_filter_tensor,
        (1, 1),
        "SAME",
        dimension_numbers=("NHWC", "HWIO", "NHWC"),
        feature_group_count=channels // partitioned_filter_tensor.shape[2],
        preferred_element_type=jnp.float32,
    )
    summed = picture_feature_maps.astype(jnp.float32) + RESIDUAL_SCALE * convolved
    tok_norm = layer_norm(summed.reshape(-1, channels), picture_token_layer_scaling).astype(
        jnp.bfloat16
    )
    lat_norm = layer_norm(summary_probes.astype(jnp.float32), summary_probe_layer_scaling).astype(
        jnp.bfloat16
    )
    tok_count = tok_norm.shape[0]
    shard_rows = asking_projection_tensor.shape[0]
    first_row = lax.axis_index("wide") * shard_rows
    lat_slice = lax.dynamic_slice_in_dim(lat_norm, first_row, shard_rows, 1)
    probe_asking_vectors = lax.psum(
        jnp.dot(lat_slice, asking_projection_tensor, preferred_element_type=jnp.float32), "wide"
    )
    rescaled_similarity_logits = (
        probe_asking_vectors.reshape(lat_count, subspace_number_overall, subspace_breadth)
        * (sharpness_coefficient / math.sqrt(subspace_breadth))[None, :, None]
    )
    key_source = jnp.concatenate([tok_norm, lat_norm], axis=0)
    zero_rows = jnp.zeros((key_source.shape[0], channels), jnp.float32)

    def add_rows(running, weight_rows):
        return running + jnp.dot(key_source, weight_rows, preferred_element_type=jnp.float32)

    def scores_of(key_part):
        return jnp.einsum(
            "lhd,thd->hlt",
            rescaled_similarity_logits,
            key_part.reshape(-1, subspace_number_overall, subspace_breadth),
            precision=lax.Precision.HIGHEST,
        )

    running = (zero_rows, zero_rows)
    weight_rows = (
        lax.all_gather(lookup_projection_tensor, "wide", axis=0, tiled=True),
        lax.all_gather(content_projection_tensor, "wide", axis=0, tiled=True),
    )
    key_proj = add_rows(running[0], weight_rows[0])
    value_proj = add_rows(running[1], weight_rows[1])
    tok_terms = softmax_terms(
        scores_of(key_proj[:tok_count]),
        value_proj[:tok_count].reshape(-1, subspace_number_overall, subspace_breadth),
    )
    lat_terms = softmax_terms(
        scores_of(key_proj[tok_count:]),
        value_proj[tok_count:].reshape(-1, subspace_number_overall, subspace_breadth),
    )
    merged = merge_all(*tok_terms)
    joint_max, joint_sum, joint_weighted = combine(merged, lat_terms)
    attention = (
        (joint_weighted / joint_sum[..., None]).transpose(1, 0, 2).reshape(lat_count, channels)
    )
    attention_low = attention.astype(jnp.bfloat16)
    out_cols = jnp.dot(attention_low, final_projection_tensor, preferred_element_type=jnp.float32)
    attended = lax.all_gather(out_cols, "wide", axis=1, tiled=True)
    new_latents = (summary_probes.astype(jnp.float32) + attended).astype(jnp.bfloat16)
    return (attended, new_latents)


def solution(mesh):
    placed = (
        P(("groups", "wide"), None, None, None),
        P(),
        P(),
        P(),
        P(),
        P("wide", None),
        P("wide", None),
        P("wide", None),
        P(None, "wide"),
        P(),
    )
    return jax.shard_map(
        per_device,
        mesh=mesh,
        in_specs=placed,
        out_specs=(P("groups", None), P("groups", None)),
        check_vma=False,
    )
```

profile of v0, /device:TPU:0, one launch (start us, length us, event | category | flops | bytes accessed | tf_op | source)
XLA Modules:
  0.0 424.6 jit_solution(6361989302038620171)
XLA Ops:
  7.2 0.7 all-gather.4.cloned.1.call-update
  8.0 0.7 all-gather.6.cloned.1.call-update
  8.7 0.0 all-reduce.3.cloned.1.call-start
  8.7 1.1 convert_reduce_fusion
  9.8 1.2 fusion.34
  11.0 1.1 fusion.36
  12.0 0.3 fusion.41
  12.3 0.2 reshape.82
  12.5 1.0 copy.42
  13.5 0.0 all-reduce.5.cloned.1.call-start
  13.5 6.2 %copy.43 = bf16[3,3,128,1536]{2,3,1,0:T(8,128)(2,1)} copy(bf16[3,3,128,1536]{3,2,1,0:T(8,128)(2,1)} %param.11) | data formatting | bytes 7077888 | tf_op args[1]
  19.7 9.5 %fusion.55 = (f32[8,10,10]{0,2,1:T(8,128)S(1)}, f32[8,10,10,1536]{3,0,2,1:T(8,128)}) fusion(bf16[3,3,128,12,128]{2,4,3,1,0:T(8,128)(2,1)} %bitcast.34, bf16[8,10,10,1536]{3,0,2,1:T(8,128)(2,1)S(1)} %copy-done.9), kind=kOutput, calls=%fused_computation.74 | convolution fusion | flops 2483453184 | bytes 10914944 | tf_op jit(solution)/shard_map/conv_general_dilated | solution.py:63
  29.2 0.1 copy.45
  29.3 0.1 copy.47
  29.5 8.7 %copy.44 = f32[8,10,10,1536]{3,2,1,0:T(8,128)} copy(f32[8,10,10,1536]{3,0,2,1:T(8,128)} %get-tuple-element.8) | data formatting | bytes 9830400 | tf_op jit(solution)/shard_map/add | solution.py:72
  38.2 0.6 multiply_reduce_fusion
  38.8 0.1 copy.48
  39.0 0.1 rsqrt.21
  39.1 6.6 %reshape.83 = f32[800,1536]{1,0:T(8,128)} reshape(f32[8,10,10,1536]{3,2,1,0:T(8,128)} %copy.44) | data formatting | bytes 9830400 | tf_op jit(solution)/shard_map/reshape | solution.py:73
  45.7 0.1 div.29
  45.9 3.1 multiply_convert_fusion
  49.0 17.4 %all-gather.4.cloned.1.call-done = bf16[1536,1536]{1,0:T(8,128)(2,1)} async-done(((bf16[96,1536]{1,0:T(8,128)(2,1)}), bf16[1536,1536]{1,0:T(8,128)(2,1)}) %all-gather.4.cloned.1.call-update) | async-done | bytes 4718608 | tf_op jit(solution)/shard_map/all_gather | solution.py:106
  66.4 8.6 %fusion.19 = f32[864,1536]{1,0:T(8,128)} fusion(bf16[1536,1536]{1,0:T(8,128)(2,1)} %all-gather.4.cloned.1.call-done, bf16[64,1536]{1,0:T(8,128)(2,1)S(1)} %fusion.36, bf16[800,1536]{1,0:T(8,128)(2,1)S(1)} %multiply_convert_fusion), kind=kOutput, calls=%fused_computation.25 | convolution fusion | flops 4082171904 | bytes 12681216 | tf_op jit(solution)/shard_map/dot_general | solution.py:94
  75.0 45.7 %all-gather.6.cloned.1.call-done = bf16[1536,1536]{1,0:T(8,128)(2,1)} async-done(((bf16[96,1536]{1,0:T(8,128)(2,1)}), bf16[1536,1536]{1,0:T(8,128)(2,1)}) %all-gather.6.cloned.1.call-update) | async-done | bytes 4718608 | tf_op jit(solution)/shard_map/all_gather | solution.py:107
  120.7 6.5 %fusion.18 = f32[864,1536]{1,0:T(8,128)S(1)} fusion(bf16[1536,1536]{1,0:T(8,128)(2,1)} %all-gather.6.cloned.1.call-done, bf16[64,1536]{1,0:T(8,128)(2,1)S(1)} %fusion.36, bf16[800,1536]{1,0:T(8,128)(2,1)S(1)} %multiply_convert_fusion), kind=kOutput, calls=%fused_computation.24 | convolution fusion | flops 4082171904 | bytes 12681216 | tf_op jit(solution)/shard_map/dot_general | solution.py:94
  127.2 2.8 slice.16
  130.0 2.5 slice.17
  132.5 6.0 %copy.50 = f32[800,1536]{0,1:T(8,128)} copy(f32[800,1536]{1,0:T(8,128)} %slice.16) | data formatting | bytes 9830400 | tf_op jit(solution)/shard_map/slice | solution.py:112
  138.5 74.2 %all-reduce.3.cloned.1.call-done = f32[64,16,96]{2,0,1:T(8,128)} async-done(((f32[64,16,96]{2,0,1:T(8,128)}), f32[64,16,96]{2,0,1:T(8,128)}) %all-reduce.3.cloned.1.call-update) | async-done | bytes 393232 | tf_op jit(solution)/shard_map/psum | solution.py:83
  212.7 8.3 %fusion.56 = (f32[16,64]{1,0:T(8,128)S(1)}, f32[16,64,800]{2,1,0:T(8,128)}) fusion(f32[800,16,96]{0,2,1:T(8,128)} %bitcast.30, f32[64,16,96]{2,0,1:T(8,128)} %all-reduce.3.cloned.1.call-done, f32[16]{0:T(128)S(1)} %broadcast_multiply_fusion.1), kind=kOutput, calls=%fused_computation.75 | convolution fusion | flops 944634880 | bytes 8589376 | tf_op jit(solution)/shard_map/lhd,thd->hlt/dot_general | solution.py:97
  221.0 32.4 %pmax.7 = f32[16,64]{1,0:T(8,128)S(1)} all-reduce(f32[16,64]{1,0:T(8,128)S(1)} %get-tuple-element.9), channel_id=1, replica_groups=mesh['groups'=2,'wide'=16] {'wide'}, use_global_device_ids=true, to_apply=%region_6.0 | all-reduce | flops 1024 | bytes 8192 | tf_op jit(solution)/shard_map/pmax | solution.py:32
  253.5 2.9 fusion.6
  256.4 30.0 %psum.23 = f32[16,64]{1,0:T(8,128)S(1)} all-reduce(f32[16,64]{1,0:T(8,128)S(1)} %get-tuple-element.5), channel_id=1, replica_groups=mesh['groups'=2,'wide'=16] {'wide'}, use_global_device_ids=true, to_apply=%region_10.0 | all-reduce | flops 1024 | bytes 8192 | tf_op jit(solution)/shard_map/psum | solution.py:34
  286.4 0.2 reshape.86
  286.6 6.0 %copy.51 = f32[800,1536]{0,1:T(8,128)} copy(f32[800,1536]{1,0:T(8,128)} %slice.17) | data formatting | bytes 9830400 | tf_op jit(solution)/shard_map/slice | solution.py:113
  292.6 11.3 %fusion.20 = f32[16,64,96]{2,1,0:T(8,128)} fusion(f32[800,16,96]{0,2,1:T(8,128)} %bitcast.31, f32[16,64,800]{2,1,0:T(8,128)} %get-tuple-element.10, f32[16,64]{1,0:T(8,128)S(1)} %get-tuple-element.9, f32[16,64]{1,0:T(8,128)S(1)} %get-tuple-element.6), kind=kOutput, calls=%fused_computation.26 | convolution fusion | flops 944635904 | bytes 8593408 | tf_op jit(solution)/shard_map/hlt,thd->hld/dot_general | solution.py:42
  303.9 0.2 reshape.87
  304.1 1.1 fusion.57
  305.2 0.1 fusion.33
  305.4 85.9 %all-reduce.5.cloned.1.call-done = f32[16,64,96]{2,1,0:T(8,128)} async-done(((f32[16,64,96]{2,1,0:T(8,128)}), f32[16,64,96]{2,1,0:T(8,128)}) %all-reduce.5.cloned.1.call-update) | async-done | bytes 393232 | tf_op jit(solution)/shard_map/psum | solution.py:34
  391.3 2.5 fusion.24
  393.8 0.2 copy.55
  393.9 0.3 convert_element_type.39
  394.2 0.2 convolution_bitcast_fusion
  394.4 22.2 %all-gather = f32[16,96,64]{1,2,0:T(8,128)S(1)} all-gather(f32[1,96,64]{1,2,0:T(8,128)S(1)} %convolution_bitcast_fusion), channel_id=1, replica_groups=mesh['groups'=2,'wide'=16] {'wide'}, dimensions={0}, use_global_device_ids=true | all-gather | bytes 417792 | tf_op jit(solution)/shard_map/all_gather | solution.py:126
  416.7 0.3 copy.56
  417.0 0.2 reshape.89
  417.2 0.8 fusion.37
  (44 shorter events, 0.3 us)
Async XLA Ops:
  7.2 4.9 %copy-start = (bf16[96,1536]{1,0:T(8,128)(2,1)S(1)}, bf16[96,1536]{1,0:T(8,128)(2,1)}, u32[]{:S(2)}) copy-start(bf16[96,1536]{1,0:T(8,128)(2,1)} %param.15) | copy-start | bytes 884740
  7.2 59.2 %all-gather.4.cloned.1.call-start = ((), (), s32[]{:S(2)}) async-start(), calls=%async_computation.1 | async-start | bytes 5013504 | tf_op jit(solution)/shard_map/all_gather | solution.py:106
  7.9 112.8 %all-gather.6.cloned.1.call-start = ((), (), s32[]{:S(2)}) async-start(), calls=%async_computation.2 | async-start | bytes 5013504 | tf_op jit(solution)/shard_map/all_gather | solution.py:107
  8.7 204.1 %all-reduce.3.cloned.1.call-start = ((), (), s32[]{:S(2)}) async-start(), calls=%async_computation | async-start | bytes 1048576 | tf_op jit(solution)/shard_map/psum | solution.py:83
  13.5 6.3 %copy-start.9 = (bf16[8,10,10,1536]{3,0,2,1:T(8,128)(2,1)S(1)}, bf16[8,10,10,1536]{3,0,2,1:T(8,128)(2,1)}, u32[]{:S(2)}) copy-start(bf16[8,10,10,1536]{3,0,2,1:T(8,128)(2,1)} %param.10) | copy-start | bytes 7372804
  13.5 377.8 %all-reduce.5.cloned.1.call-start = ((), (), s32[]{:S(2)}) async-start(), calls=%async_computation.3 | async-start | bytes 1048576 | tf_op jit(solution)/shard_map/psum | solution.py:34
  29.3 8.8 %slice-start = ((s8[4915200]{0:T(1024)(128)(4,1)}), s8[720896]{0:T(1024)(128)(4,1)S(1)}, s32[]{:S(2)}) async-start(s8[4915200]{0:T(1024)(128)(4,1)} %bitcast.32), calls=%async_computation.4 | async-start | bytes 1441792
  29.5 8.7 %slice-start.1 = ((s8[4915200]{0:T(1024)(128)(4,1)}), s8[4194304]{0:T(1024)(128)(4,1)S(1)}, s32[]{:S(2)}) async-start(s8[4915200]{0:T(1024)(128)(4,1)} %bitcast.32), calls=%async_computation.5 | async-start | bytes 8388608
  39.1 6.8 %copy-start.10 = (f32[16]{0:T(128)S(1)}, f32[16]{0:T(128)}, u32[]{:S(2)}) copy-start(f32[16]{0:T(128)} %param.19) | copy-start | bytes 196
  39.1 6.8 %copy-start.8 = (f32[1536]{0:T(1024)S(1)}, f32[1536]{0:T(1024)}, u32[]{:S(2)}) copy-start(f32[1536]{0:T(1024)} %param.12) | copy-start | bytes 18436
  120.7 6.5 %copy-start.2 = (f32[864,1536]{1,0:T(8,128)S(1)}, f32[864,1536]{1,0:T(8,128)}, u32[]{:S(2)}) copy-start(f32[864,1536]{1,0:T(8,128)} %fusion.19) | copy-start | bytes 15925252
  127.2 5.4 %copy-start.3 = (f32[864,1536]{1,0:T(8,128)}, f32[864,1536]{1,0:T(8,128)S(1)}, u32[]{:S(2)}) copy-start(f32[864,1536]{1,0:T(8,128)S(1)} %fusion.18) | copy-start | bytes 15925252
  212.7 73.7 %slice-start.2 = ((f32[864,1536]{1,0:T(8,128)}), f32[64,1536]{1,0:T(8,128)S(1)}, s32[]{:S(2)}) async-start(f32[864,1536]{1,0:T(8,128)} %fusion.19), calls=%async_computation.6 | async-start | bytes 786432 | tf_op jit(solution)/shard_map/slice | solution.py:116
  292.5 11.3 %slice-start.3 = ((f32[864,1536]{1,0:T(8,128)}), f32[64,1536]{1,0:T(8,128)S(1)}, s32[]{:S(2)}) async-start(f32[864,1536]{1,0:T(8,128)} %copy-done.3), calls=%async_computation.7 | async-start | bytes 786432 | tf_op jit(solution)/shard_map/slice | solution.py:117
  292.6 11.5 %copy-start.5 = (f32[64,16,96]{2,0,1:T(8,128)S(1)}, f32[64,16,96]{2,0,1:T(8,128)}, u32[]{:S(2)}) copy-start(f32[64,16,96]{2,0,1:T(8,128)} %all-reduce.3.cloned.1.call-done) | copy-start | bytes 1179652
  303.8 90.4 %copy-start.7 = (bf16[1536,96]{0,1:T(8,128)(2,1)S(1)}, bf16[1536,96]{0,1:T(8,128)(2,1)}, u32[]{:S(2)}) copy-start(bf16[1536,96]{0,1:T(8,128)(2,1)} %param.18) | copy-start | bytes 884740
  303.9 113.4 %copy-start.4 = (bf16[64,1536]{1,0:T(8,128)(2,1)S(1)}, bf16[64,1536]{1,0:T(8,128)(2,1)}, u32[]{:S(2)}) copy-start(bf16[64,1536]{1,0:T(8,128)(2,1)} %param.13) | copy-start | bytes 589828
  303.9 114.2 %copy-start.1 = (bf16[96,1536]{1,0:T(8,128)(2,1)S(1)}, bf16[96,1536]{1,0:T(8,128)(2,1)}, u32[]{:S(2)}) copy-start(bf16[96,1536]{1,0:T(8,128)(2,1)} %param.15) | copy-start | bytes 884740
  417.2 0.8 copy-start.6
Sparse Core Ops, SparseCore 0:
  10.3 56.0 all-gather.3
  68.7 51.9 all-gather.5
  124.1 88.5 all-reduce.2
  304.0 87.2 all-reduce.4
where the time goes:
time: 425 us
  waiting for transfers between devices  225 us (53%)
  blocking collectives  84.7 us (20%)
  matrix products  48.2 us (11%)
  local copies, waits for them, and re-layouts  42 us (10%)
  between operations  14.1 us (3%)
  other arithmetic  10.9 us (3%)
    psum x1, waiting for transfers between devices, merge_all(): lax.psum((row_sum * factor, weighted * factor[..., None]), 'wide')  85.9 us
    psum x1, waiting for transfers between devices, per_device(): lax.psum(jnp.dot(lat_slice, asking_projection_tensor, preferred_element_t...  74.2 us
    all_gather x1, waiting for transfers between devices, per_device(): lax.all_gather(content_projection_tensor, 'wide', axis=0, tiled=True)  45.7 us
    pmax x1, blocking collectives, merge_all(): joint_max = lax.pmax(row_max, 'wide')  32.4 us
    psum x1, blocking collectives, merge_all(): lax.psum((row_sum * factor, weighted * factor[..., None]), 'wide')  30 us
    all_gather x1, blocking collectives, per_device(): attended = lax.all_gather(out_cols, 'wide', axis=1, tiled=True)  22.2 us
    all_gather x1, waiting for transfers between devices, per_device(): lax.all_gather(lookup_projection_tensor, 'wide', axis=0, tiled=True)  17.4 us
    dot_general x2, matrix products, add_rows(): jnp.dot(key_source, weight_rows, preferred_element_type=jnp.float32)  15 us
  transfers between devices with their start and end apart: 4, of which 4 were waited for; matrix products, arithmetic and copies ran while one was open for 16% of the time, Pallas kernels for 0%

commit v1 on v0

v1 whole, which is shorter than its diff:
```python
import functools
import math

import jax
import jax.numpy as jnp
from jax import lax
from jax.experimental import pallas as pl
from jax.experimental.pallas import tpu as pltpu
from jax.sharding import PartitionSpec as P

RESIDUAL_SCALE = 0.2
EPSILON = 1e-06
LANES = 128
NT = (((1,), (1,)), ((), ()))


def layer_norm(values, gain):
    center = values - jnp.mean(values, axis=-1, keepdims=True)
    spread = jnp.mean(center * center, axis=-1, keepdims=True)
    return center * lax.rsqrt(spread + EPSILON) * gain


def window(head, breadth):
    start = head * breadth // LANES * LANES
    stop = -(-(head + 1) * breadth // LANES) * LANES
    return start, stop - start


def head_mask(head, breadth, shape):
    start, width = window(head, breadth)
    lane = lax.broadcasted_iota(jnp.int32, shape, len(shape) - 1) + start
    return (lane >= head * breadth) & (lane < (head + 1) * breadth)


def halves(values):
    high = values.astype(jnp.bfloat16)
    low = (values - high.astype(jnp.float32)).astype(jnp.bfloat16)
    return high, low


def mixer(
    n, heads, tok_count,
    tok_ref, lat_own_ref, lat_slice_ref, probes_ref, sharp_ref,
    wq_ref, wk_ref, wv_ref, wo_ref,
    attended_ref, new_ref,
    gathered, qpart, qrecv, qall, queries, source, u_high, u_low,
    wsum, part, received, att_all, att_low, cols_all,
    z_send, y_send, core_send, w_recv, swap_send, swap_recv,
):
    channels = sharp_ref.shape[1]
    breadth = channels // heads
    lats = probes_ref.shape[0]
    rows = lats // n
    shard = wk_ref.shape[0]
    line = n // 4
    me = lax.axis_index("wide")
    core = lax.rem(me, 2)
    side = lax.rem(me // 2, 2)
    at = me // 4
    weights = (wk_ref, wv_ref)

    def place(a, b, c):
        return a * 4 + b * 2 + c

    def remote(src, dst, send, recv, target):
        return pltpu.make_async_remote_copy(
            src_ref=src, dst_ref=dst, send_sem=send, recv_sem=recv,
            device_id={"wide": target}, device_id_type=pl.DeviceIdType.MESH,
        )

    def ring(k):
        return lax.rem(me + k, n)

    def back(k):
        return lax.rem(me + n - k, n)

    def loop(count, body):
        def step(k, carry):
            body(k)
            return carry
        lax.fori_loop(1, count, step, 0)

    def swap(slot, src_of, dst, target, owner):
        return remote(
            src_of(target), dst.at[owner], swap_send.at[slot, target], swap_recv.at[slot, owner], target
        )

    def swap_start(slot, src_of, dst):
        loop(n, lambda k: swap(slot, src_of, dst, ring(k), me).start())

    def swap_wait(slot, src_of, dst):
        loop(n, lambda k: swap(slot, src_of, dst, ring(k), me).wait_send())
        loop(n, lambda k: swap(slot, src_of, dst, me, back(k)).wait_recv())

    def along(w, k):
        return remote(
            weights[w], gathered.at[w, me], z_send.at[w, k], w_recv.at[w, me],
            place(lax.rem(at + k, line), side, core),
        )

    def across(w, a):
        owner = place(a, side, core)
        return remote(
            gathered.at[w, owner], gathered.at[w, owner], y_send.at[w, a], w_recv.at[w, owner],
            place(at, 1 - side, core),
        )

    def over(w, a, b):
        owner = place(a, b, core)
        return remote(
            gathered.at[w, owner], gathered.at[w, owner], core_send.at[w, a * 2 + b],
            w_recv.at[w, owner], place(at, side, 1 - core),
        )

    def arrival(w, owner):
        remote(
            gathered.at[w, owner], gathered.at[w, owner], z_send.at[w, 0], w_recv.at[w, owner],
            place(at, side, 1 - core),
        ).wait_recv()

    def line_step(w, k):
        a = lax.rem(at + line - k, line)
        arrival(w, place(a, side, core))
        across(w, a).start()
        over(w, a, side).start()

    def far_step(w, k):
        a = lax.rem(at + line - k, line)
        arrival(w, place(a, 1 - side, core))
        over(w, a, 1 - side).start()

    def core_step(w, k):
        arrival(w, place(k // 2, lax.rem(k, 2), 1 - core))

    def finish_sends(w):
        def one(k, carry):
            across(w, k).wait_send()
            over(w, k, 0).wait_send()
            over(w, k, 1).wait_send()
            return carry
        loop(line, lambda k: along(w, k).wait_send())
        lax.fori_loop(0, line, one, 0)

    def each(count, body):
        def step(k, carry):
            body(k)
            return carry
        lax.fori_loop(0, count, step, 0)

    barrier = pltpu.get_barrier_semaphore()
    loop(n, lambda k: pl.semaphore_signal(
        barrier, inc=1, device_id={"wide": ring(k)}, device_id_type=pl.DeviceIdType.MESH))
    pl.semaphore_wait(barrier, n - 1)

    partial = jnp.dot(lat_slice_ref[...], wq_ref[...], preferred_element_type=jnp.float32)
    for j in range(n):
        qpart[j] = partial[j * rows:(j + 1) * rows]
    qrecv[me] = qpart[me]
    swap_start(0, lambda j: qpart.at[j], qrecv)
    for w in range(2):
        gathered[w, me] = weights[w][...]
        loop(line, lambda k: along(w, k).start())
        across(w, at).start()
        over(w, at, side).start()

    source[:tok_count] = tok_ref[...]
    source[tok_count:] = lat_own_ref[...]

    swap_wait(0, lambda j: qpart.at[j], qrecv)
    qall[me] = jnp.sum(qrecv[...], axis=0) * sharp_ref[...]
    swap_start(1, lambda j: qall.at[me], qall)

    loop(line, lambda k: line_step(0, k))
    each(line, lambda k: far_step(0, k))
    loop(line, lambda k: line_step(1, k))
    swap_wait(1, lambda j: qall.at[me], qall)
    for j in range(n):
        queries[j * rows:(j + 1) * rows] = qall[j]
    each(n // 2, lambda k: core_step(0, k))

    total = source.shape[0]
    per_block = max(1, min(heads, 256 // lats))
    lane = lax.broadcasted_iota(jnp.int32, (lats, LANES), 1)
    stat_max = jnp.zeros((lats, LANES), jnp.float32)
    stat_sum = jnp.zeros((lats, LANES), jnp.float32)
    for first in range(0, heads, per_block):
        folded = []
        for head in range(first, first + per_block):
            start, width = window(head, breadth)
            part_q = queries[:, start:start + width]
            part_q = jnp.where(head_mask(head, breadth, part_q.shape), part_q, 0.0)
            both = jnp.concatenate(halves(part_q), axis=0)
            look = gathered[0, :, :, start:start + width].astype(jnp.bfloat16)
            look = look.reshape(n * shard, width)
            raw = lax.dot_general(both, look, NT, preferred_element_type=jnp.float32)
            folded.append(raw[:lats] + raw[lats:])
        high, low = halves(jnp.concatenate(folded, axis=0))
        scores = lax.dot_general(high, source[...], NT, preferred_element_type=jnp.float32)
        scores += lax.dot_general(low, source[...], NT, preferred_element_type=jnp.float32)
        column = lax.broadcasted_iota(jnp.int32, scores.shape, 1)
        scores = jnp.where(column < tok_count + rows, scores, -jnp.inf)
        row_max = jnp.max(scores, axis=1, keepdims=True)
        terms = jnp.exp(scores - row_max).astype(jnp.bfloat16)
        row_sum = jnp.sum(terms.astype(jnp.float32), axis=1, keepdims=True)
        mixed = jnp.dot(terms, source[...], preferred_element_type=jnp.float32)
        high, low = halves(mixed)
        u_high[first * lats:(first + per_block) * lats] = high
        u_low[first * lats:(first + per_block) * lats] = low
        for i in range(per_block):
            stat_max = jnp.where(lane == first + i, row_max[i * lats:(i + 1) * lats], stat_max)
            stat_sum = jnp.where(lane == first + i, row_sum[i * lats:(i + 1) * lats], stat_sum)
        if first == 0:
            each(line, lambda k: far_step(1, k))
    each(n // 2, lambda k: core_step(1, k))

    wsum[...] = jnp.zeros_like(wsum)
    for head in range(heads):
        start, width = window(head, breadth)
        both = jnp.concatenate(
            [u_high[head * lats:(head + 1) * lats], u_low[head * lats:(head + 1) * lats]], axis=0
        )
        content = gathered[1, :, :, start:start + width].astype(jnp.bfloat16)
        raw = jnp.dot(both, content.reshape(n * shard, width), preferred_element_type=jnp.float32)
        raw = raw[:lats] + raw[lats:]
        wsum[:, start:start + width] += jnp.where(head_mask(head, breadth, raw.shape), raw, 0.0)
    for j in range(n):
        cut = slice(j * rows, (j + 1) * rows)
        part[j, :, :channels] = wsum[cut]
        part[j, :, channels:channels + LANES] = stat_max[cut]
        part[j, :, channels + LANES:] = stat_sum[cut]
    received[me] = part[me]
    swap_start(2, lambda j: part.at[j], received)
    swap_wait(2, lambda j: part.at[j], received)

    maxima = received[:, :, channels:channels + LANES]
    factor = jnp.exp(maxima - jnp.max(maxima, axis=0, keepdims=True))
    joint = jnp.sum(received[:, :, channels + LANES:] * factor, axis=0, keepdims=True)
    factor = factor / jnp.where(joint > 0.0, joint, 1.0)
    att_all[me] = jnp.zeros((rows, channels), jnp.float32)
    for head in range(heads):
        start, width = window(head, breadth)
        scaled = received[:, :, start:start + width] * factor[:, :, head:head + 1]
        scaled = jnp.sum(scaled, axis=0)
        keep = head_mask(head, breadth, scaled.shape)
        att_all[me, :, start:start + width] += jnp.where(keep, scaled, 0.0)
    swap_start(3, lambda j: att_all.at[me], att_all)
    swap_wait(3, lambda j: att_all.at[me], att_all)
    for j in range(n):
        wsum[j * rows:(j + 1) * rows] = att_all[j]
    att_low[...] = wsum[...].astype(jnp.bfloat16)
    cols_all[me] = jnp.dot(att_low[...], wo_ref[...], preferred_element_type=jnp.float32)
    swap_start(4, lambda j: cols_all.at[me], cols_all)
    swap_wait(4, lambda j: cols_all.at[me], cols_all)
    wide = wo_ref.shape[1]
    for j in range(n):
        attended_ref[:, j * wide:(j + 1) * wide] = cols_all[j]
    new_ref[...] = (probes_ref[...].astype(jnp.float32) + attended_ref[...]).astype(jnp.bfloat16)
    finish_sends(0)
    finish_sends(1)


def per_device(
    n,
    picture_feature_maps,
    partitioned_filter_tensor,
    picture_token_layer_scaling,
    summary_probes,
    summary_probe_layer_scaling,
    asking_projection_tensor,
    lookup_projection_tensor,
    content_projection_tensor,
    final_projection_tensor,
    sharpness_coefficient,
):
    channels = picture_feature_maps.shape[3]
    heads = sharpness_coefficient.shape[0]
    breadth = channels // heads
    lats = summary_probes.shape[0]
    activated = jax.nn.gelu(picture_feature_maps.astype(jnp.float32)).astype(jnp.bfloat16)
    convolved = lax.conv_general_dilated(
        activated,
        partitioned_filter_tensor,
        (1, 1),
        "SAME",
        dimension_numbers=("NHWC", "HWIO", "NHWC"),
        feature_group_count=channels // partitioned_filter_tensor.shape[2],
        preferred_element_type=jnp.float32,
    )
    summed = picture_feature_maps.astype(jnp.float32) + RESIDUAL_SCALE * convolved
    tok_norm = layer_norm(summed.reshape(-1, channels), picture_token_layer_scaling).astype(
        jnp.bfloat16
    )
    lat_norm = layer_norm(summary_probes.astype(jnp.float32), summary_probe_layer_scaling).astype(
        jnp.bfloat16
    )
    tok_count = tok_norm.shape[0]
    shard = asking_projection_tensor.shape[0]
    rows = lats // n
    me = lax.axis_index("wide")
    lat_slice = lax.dynamic_slice_in_dim(lat_norm, me * shard, shard, 1)
    lat_own = lax.dynamic_slice_in_dim(lat_norm, me * rows, rows, 0)
    extra = -(-rows // 16) * 16
    lat_own = jnp.pad(lat_own, ((0, extra - rows), (0, 0)))
    sharp = jnp.repeat(sharpness_coefficient / math.sqrt(breadth), breadth)[None, :]
    lookup, content = lookup_projection_tensor, content_projection_tensor
    wire = jnp.bfloat16 if shard % 16 == 0 else jnp.float32
    lookup, content = lookup.astype(wire), content.astype(wire)
    vmem = pl.BlockSpec(memory_space=pltpu.VMEM)
    f32, bf16 = jnp.float32, jnp.bfloat16
    width = final_projection_tensor.shape[1]
    line = n // 4
    return pl.pallas_call(
        functools.partial(mixer, n, heads, tok_count),
        out_shape=(
            jax.ShapeDtypeStruct((lats, channels), f32),
            jax.ShapeDtypeStruct((lats, channels), bf16),
        ),
        in_specs=[vmem] * 9,
        out_specs=(vmem, vmem),
        scratch_shapes=[
            pltpu.VMEM((2, n, shard, channels), wire),
            pltpu.VMEM((n, rows, channels), f32),
            pltpu.VMEM((n, rows, channels), f32),
            pltpu.VMEM((n, rows, channels), f32),
            pltpu.VMEM((lats, channels), f32),
            pltpu.VMEM((tok_count + extra, channels), bf16),
            pltpu.VMEM((heads * lats, channels), bf16),
            pltpu.VMEM((heads * lats, channels), bf16),
            pltpu.VMEM((lats, channels), f32),
            pltpu.VMEM((n, rows, channels + 2 * LANES), f32),
            pltpu.VMEM((n, rows, channels + 2 * LANES), f32),
            pltpu.VMEM((n, rows, channels), f32),
            pltpu.VMEM((lats, channels), bf16),
            pltpu.VMEM((n, lats, width), f32),
            pltpu.SemaphoreType.DMA((2, line)),
            pltpu.SemaphoreType.DMA((2, line)),
            pltpu.SemaphoreType.DMA((2, 2 * line)),
            pltpu.SemaphoreType.DMA((2, n)),
            pltpu.SemaphoreType.DMA((5, n)),
            pltpu.SemaphoreType.DMA((5, n)),
        ],
        compiler_params=pltpu.CompilerParams(
            collective_id=0, has_side_effects=True, vmem_limit_bytes=56 * 1024 * 1024
        ),
    )(
        tok_norm, lat_own, lat_slice, summary_probes, sharp,
        asking_projection_tensor, lookup, content, final_projection_tensor,
    )


def solution(mesh):
    placed = (
        P(("groups", "wide"), None, None, None),
        P(),
        P(),
        P(),
        P(),
        P("wide", None),
        P("wide", None),
        P("wide", None),
        P(None, "wide"),
        P(),
    )
    return jax.shard_map(
        functools.partial(per_device, mesh.shape["wide"]),
        mesh=mesh,
        in_specs=placed,
        out_specs=(P("groups", None), P("groups", None)),
        check_vma=False,
    )
```

time: 425 us -> 187 us (0.44)
  waiting for transfers between devices: 225 us -> 0 us
  Pallas kernels: 0 us -> 134 us
  blocking collectives: 84.7 us -> 0 us
  matrix products: 48.2 us -> 10.3 us
  local copies, waits for them, and re-layouts: 42 us -> 28.2 us
  between operations: 14.1 us -> 0.74 us
    psum x2 -> x0, waiting for transfers between devices: 160 us -> none  [the longest x1 85.9 us: merge_all(): lax.psum((row_sum * factor, weighted * factor[..., None]), 'wide')]
    pallas_call x0 -> x1, Pallas kernels: none -> 134 us  [per_device(): pl.pallas_call(functools.partial(mixer, n, heads, tok_count), out_shape=(...]
    all_gather x2 -> x0, waiting for transfers between devices: 63.1 us -> none  [the longest x1 45.7 us: per_device(): lax.all_gather(content_projection_tensor, 'wide', axis=0, tiled=True)]
    dot_general x8 -> x0, matrix products: 38.7 us -> none  [the longest x2 15 us: add_rows(): jnp.dot(key_source, weight_rows, preferred_element_type=jnp.float32)]
    pmax x1 -> x0, blocking collectives: 32.4 us -> none  [merge_all(): joint_max = lax.pmax(row_max, 'wide')]
    psum x1 -> x0, blocking collectives: 30 us -> none  [merge_all(): lax.psum((row_sum * factor, weighted * factor[..., None]), 'wide')]
    all_gather x1 -> x0, blocking collectives: 22.2 us -> none  [per_device(): attended = lax.all_gather(out_cols, 'wide', axis=1, tiled=True)]
    slice x8 -> x0, local copies, waits for them, and re-layouts: 17.3 us -> none  [the longest x2 8.8 us: per_device(): key_proj[:tok_count]]
  transfers between devices with their start and end apart: 4 -> 0, of which waited for: 4 -> 0; matrix products, arithmetic and copies ran while one was open for 16% -> 0% of each run, Pallas kernels for 0% -> 0%
where the time goes in v1:
time: 187 us; the launch traced here: 185 us
  Pallas kernels  134 us (72%)
  local copies, waits for them, and re-layouts  28.2 us (15%)
  other arithmetic  10.9 us (6%)
  matrix products  10.3 us (6%)
    pallas_call x1, Pallas kernels, per_device(): pl.pallas_call(functools.partial(mixer, n, heads, tok_count), out_shape=(...  134 us
    conv_general_dilated x1, matrix products, per_device(): lax.conv_general_dilated(activated, partitioned_filter_tensor, (1, 1), 'S...  10.3 us
    unnamed x10, local copies, waits for them, and re-layouts  8.84 us
    add x1, local copies, waits for them, and re-layouts, per_device(): picture_feature_maps.astype(jnp.float32) + RESIDUAL_SCALE * convolved  8.51 us
    reshape x1, local copies, waits for them, and re-layouts, per_device(): summed.reshape(-1, channels)  7.23 us
    convert_element_type x1, other arithmetic, per_device(): layer_norm(summed.reshape(-1, channels), picture_token_layer_scaling)  4.52 us
    reduce_sum x2, other arithmetic, layer_norm(): spread = jnp.mean(center * center, axis=-1, keepdims=True)  4.19 us

profile of v1, /device:TPU:0, one launch (start us, length us, event | category | flops | bytes accessed | tf_op | source)
XLA Modules:
  0.0 184.6 jit_solution(12963413096902444500)
XLA Ops:
  0.6 1.1 convert_reduce_fusion
  1.7 1.2 fusion.17
  2.9 1.1 fusion.19
  4.0 0.6 pad.4.lat_own_ref
  4.6 0.7 constant_dynamic-slice_fusion.lat_slice_ref
  5.3 4.5 %copy.24 = bf16[3,3,128,1536]{2,3,1,0:T(8,128)(2,1)S(1)} copy(bf16[3,3,128,1536]{3,2,1,0:T(8,128)(2,1)} %param.11) | data formatting | bytes 7077888 | tf_op args[1]
  9.8 10.3 %fusion.24 = (f32[8,10,10]{0,2,1:T(8,128)}, f32[8,10,10,1536]{3,0,2,1:T(8,128)}) fusion(bf16[3,3,128,12,128]{2,4,3,1,0:T(8,128)(2,1)S(1)} %bitcast.11, bf16[8,10,10,1536]{3,0,2,1:T(8,128)(2,1)} %param.10), kind=kOutput, calls=%fused_computation.37 | convolution fusion | flops 2483453184 | bytes 10914944 | tf_op jit(solution)/shard_map/conv_general_dilated | solution.py:280
  20.1 1.0 copy.26
  21.1 0.1 copy.28
  21.3 3.0 %multiply_reduce_fusion = f32[8,10,10]{0,2,1:T(8,128)S(1)} fusion(f32[8,10,10,1536]{3,0,2,1:T(8,128)} %get-tuple-element.3, f32[8,10,10]{0,2,1:T(8,128)S(1)} %copy.28), kind=kLoop, calls=%fused_computation.12 | loop fusion | flops 3685600 | bytes 4921600 | tf_op jit(solution)/shard_map/reduce_sum | solution.py:19
  24.3 0.1 copy.29
  24.5 0.1 rsqrt.20
  24.6 8.5 %copy.25 = f32[8,10,10,1536]{3,2,1,0:T(8,128)} copy(f32[8,10,10,1536]{3,0,2,1:T(8,128)} %get-tuple-element.3) | data formatting | bytes 9830400 | tf_op jit(solution)/shard_map/add | solution.py:289
  33.1 0.0 copy-start.1
  33.1 7.2 %reshape.58 = f32[800,1536]{1,0:T(8,128)} reshape(f32[8,10,10,1536]{3,2,1,0:T(8,128)} %copy.25) | data formatting | bytes 9830400 | tf_op jit(solution)/shard_map/reshape | solution.py:290
  40.3 0.0 copy-start
  40.3 0.0 copy-start.2
  40.4 0.1 div.18
  40.5 0.0 copy-done.1
  40.5 4.5 %multiply_convert_fusion.tok_ref = bf16[800,1536]{1,0:T(8,128)(2,1)} fusion(f32[800,1536]{1,0:T(8,128)} %reshape.58, f32[1536]{0:T(1024)S(1)} %copy-done.1, f32[800]{0:T(1024)S(1)} %rsqrt.20, f32[800]{0:T(1024)S(1)} %div.18), kind=kLoop, calls=%fused_computation.11 | loop fusion | flops 4915200 | bytes 7385344 | tf_op jit(solution)/shard_map/convert_element_type | solution.py:290
  45.0 0.0 copy-done
  45.0 0.9 copy.31.wo_ref
  45.9 0.0 copy-done.2
  46.0 0.1 broadcast_in_dim.2
  46.0 0.7 broadcast_in_dim_reshape.3.sharp_ref
  46.7 134.5 %shard_map.116 = (f32[64,1536]{1,0:T(8,128)}, bf16[64,1536]{1,0:T(8,128)(2,1)}) custom-call(bf16[800,1536]{1,0:T(8,128)(2,1)} %multiply_convert_fusion.tok_ref, bf16[16,1536]{1,0:T(8,128)(2,1)} %pad.4.lat_own_ref, bf16[64,96]{1,0:T(8,128)(2,1)} %constant_dynamic-slice_fusion.lat_slice_ref, bf16[64,1536]{1,0:T(8,128)(2,1)} %probes_ref.1, ...), custom_call_target="tpu_custom_call" | custom-call | tf_op jit(solution)/shard_map/pallas_call | solution.py:312
  181.2 1.8 copy.34
  182.9 1.6 copy.35
  (8 shorter events, 0.1 us)
Async XLA Ops:
  33.1 7.4 %copy-start.1 = (f32[1536]{0:T(1024)S(1)}, f32[1536]{0:T(1024)}, u32[]{:S(2)}) copy-start(f32[1536]{0:T(1024)} %param.12) | copy-start | bytes 18436
  40.3 4.7 %copy-start = (bf16[1536,96]{0,1:T(8,128)(2,1)S(1)}, bf16[1536,96]{0,1:T(8,128)(2,1)}, u32[]{:S(2)}) copy-start(bf16[1536,96]{0,1:T(8,128)(2,1)} %param.18) | copy-start | bytes 884740
  40.3 5.6 %copy-start.2 = (f32[16]{0:T(128)S(1)}, f32[16]{0:T(128)}, u32[]{:S(2)}) copy-start(f32[16]{0:T(128)} %param.19) | copy-start | bytes 196

commit v2 on v1

--- a/solution.py
+++ b/solution.py
@@ -3,6 +3,7 @@
 
 import jax
 import jax.numpy as jnp
+import numpy as np
 from jax import lax
 from jax.experimental import pallas as pl
 from jax.experimental.pallas import tpu as pltpu
@@ -39,12 +40,13 @@
 
 
 def mixer(
-    n, heads, tok_count,
-    tok_ref, lat_own_ref, lat_slice_ref, probes_ref, sharp_ref,
+    n, heads,
+    maps_ref, filter_ref, gain_ref, pick_ref, lat_own_ref, lat_slice_ref, probes_ref, sharp_ref,
     wq_ref, wk_ref, wv_ref, wo_ref,
     attended_ref, new_ref,
     gathered, qpart, qrecv, qall, queries, source, u_high, u_low,
     wsum, part, received, att_all, att_low, cols_all,
+    plain, act, summed,
     z_send, y_send, core_send, w_recv, swap_send, swap_recv,
 ):
     channels = sharp_ref.shape[1]
@@ -157,28 +159,83 @@
         qpart[j] = partial[j * rows:(j + 1) * rows]
     qrecv[me] = qpart[me]
     swap_start(0, lambda j: qpart.at[j], qrecv)
-    for w in range(2):
+
+    def send_own(w):
         gathered[w, me] = weights[w][...]
         loop(line, lambda k: along(w, k).start())
         across(w, at).start()
         over(w, at, side).start()
 
-    source[:tok_count] = tok_ref[...]
+    send_own(0)
+    frames, high_side, wide_side = maps_ref.shape[:3]
+    group = filter_ref.shape[0] // 9
+    at_once = plain.shape[0]
+    pitch = plain.shape[2]
+    flat = high_side * pitch
+    steps = frames // at_once
+    packed = pick_ref.shape[0]
+    real = at_once * high_side * wide_side
+    tok_count = steps * packed
+    plain[...] = jnp.zeros_like(plain)
+    act[...] = jnp.zeros_like(act)
     source[tok_count:] = lat_own_ref[...]
+
+    def convolve(i):
+        for f in range(at_once):
+            plain[f, :, :wide_side] = maps_ref[i * at_once + f].astype(jnp.float32)
+            g = jax.nn.gelu(plain[f]).reshape(flat, channels)
+            act[f, 0, pitch:pitch + flat] = pltpu.roll(g, 1, 0).astype(jnp.bfloat16)
+            act[f, 1, pitch:pitch + flat] = g.astype(jnp.bfloat16)
+            act[f, 2, pitch:pitch + flat] = pltpu.roll(g, flat - 1, 0).astype(jnp.bfloat16)
+        for c in range(channels // group):
+            cut = slice(c * group, (c + 1) * group)
+            taps = jnp.concatenate([
+                jnp.concatenate([
+                    act[f, dx, dy * pitch:dy * pitch + flat, cut]
+                    for dy in range(3) for dx in range(3)
+                ], axis=1)
+                for f in range(at_once)
+            ], axis=0)
+            summed[:, cut] = jnp.dot(
+                taps, filter_ref[:, cut], preferred_element_type=jnp.float32)
+        normed = []
+        for f in range(at_once):
+            rows_of = slice(f * flat, (f + 1) * flat)
+            value = plain[f].reshape(flat, channels) + RESIDUAL_SCALE * summed[rows_of]
+            normed.append(layer_norm(value, gain_ref[...]).astype(jnp.bfloat16))
+        dense = jnp.dot(
+            pick_ref[...], jnp.concatenate(normed, axis=0), preferred_element_type=jnp.float32)
+        where = pl.multiple_of(i * packed, 16)
+        source[pl.ds(where, packed)] = dense.astype(jnp.bfloat16)
+
+    def conv_and_pass(i, carry):
+        convolve(i)
+
+        @pl.when((i >= 1) & (i < line))
+        def _():
+            line_step(0, i)
+        return carry
+
+    lax.fori_loop(0, steps, conv_and_pass, 0)
+
+    def pass_on(k, carry):
+        line_step(0, k)
+        return carry
+
+    lax.fori_loop(min(steps, line), line, pass_on, 0)
+    send_own(1)
 
     swap_wait(0, lambda j: qpart.at[j], qrecv)
     qall[me] = jnp.sum(qrecv[...], axis=0) * sharp_ref[...]
     swap_start(1, lambda j: qall.at[me], qall)
 
-    loop(line, lambda k: line_step(0, k))
     each(line, lambda k: far_step(0, k))
-    loop(line, lambda k: line_step(1, k))
     swap_wait(1, lambda j: qall.at[me], qall)
     for j in range(n):
         queries[j * rows:(j + 1) * rows] = qall[j]
     each(n // 2, lambda k: core_step(0, k))
-
-    total = source.shape[0]
+    loop(line, lambda k: line_step(1, k))
+
     per_block = max(1, min(heads, 256 // lats))
     lane = lax.broadcasted_iota(jnp.int32, (lats, LANES), 1)
     stat_max = jnp.zeros((lats, LANES), jnp.float32)
@@ -198,7 +255,10 @@
         scores = lax.dot_general(high, source[...], NT, preferred_element_type=jnp.float32)
         scores += lax.dot_general(low, source[...], NT, preferred_element_type=jnp.float32)
         column = lax.broadcasted_iota(jnp.int32, scores.shape, 1)
-        scores = jnp.where(column < tok_count + rows, scores, -jnp.inf)
+        live = (column >= tok_count) & (column < tok_count + rows)
+        for i in range(steps):
+            live |= (column >= i * packed) & (column < i * packed + real)
+        scores = jnp.where(live, scores, -jnp.inf)
         row_max = jnp.max(scores, axis=1, keepdims=True)
         terms = jnp.exp(scores - row_max).astype(jnp.bfloat16)
         row_sum = jnp.sum(terms.astype(jnp.float32), axis=1, keepdims=True)
@@ -276,24 +336,20 @@
     heads = sharpness_coefficient.shape[0]
     breadth = channels // heads
     lats = summary_probes.shape[0]
-    activated = jax.nn.gelu(picture_feature_maps.astype(jnp.float32)).astype(jnp.bfloat16)
-    convolved = lax.conv_general_dilated(
-        activated,
-        partitioned_filter_tensor,
-        (1, 1),
-        "SAME",
-        dimension_numbers=("NHWC", "HWIO", "NHWC"),
-        feature_group_count=channels // partitioned_filter_tensor.shape[2],
-        preferred_element_type=jnp.float32,
-    )
-    summed = picture_feature_maps.astype(jnp.float32) + RESIDUAL_SCALE * convolved
-    tok_norm = layer_norm(summed.reshape(-1, channels), picture_token_layer_scaling).astype(
-        jnp.bfloat16
-    )
+    frames, high_side, wide_side, _ = picture_feature_maps.shape
+    at_once = 2 if frames % 2 == 0 else 1
+    pitch = -(-(wide_side + 1) // 16) * 16
+    flat = high_side * pitch
+    real = at_once * high_side * wide_side
+    packed = -(-real // 16) * 16
+    pick = np.zeros((packed, at_once * flat), np.float32)
+    for r in range(real):
+        pick[r, r // wide_side * pitch + r % wide_side] = 1.0
+    filters = partitioned_filter_tensor.reshape(-1, channels)
+    tok_count = frames // at_once * packed
     lat_norm = layer_norm(summary_probes.astype(jnp.float32), summary_probe_layer_scaling).astype(
         jnp.bfloat16
     )
-    tok_count = tok_norm.shape[0]
     shard = asking_projection_tensor.shape[0]
     rows = lats // n
     me = lax.axis_index("wide")
@@ -310,12 +366,12 @@
     width = final_projection_tensor.shape[1]
     line = n // 4
     return pl.pallas_call(
-        functools.partial(mixer, n, heads, tok_count),
+        functools.partial(mixer, n, heads),
         out_shape=(
             jax.ShapeDtypeStruct((lats, channels), f32),
             jax.ShapeDtypeStruct((lats, channels), bf16),
         ),
-        in_specs=[vmem] * 9,
+        in_specs=[vmem] * 12,
         out_specs=(vmem, vmem),
         scratch_shapes=[
             pltpu.VMEM((2, n, shard, channels), wire),
@@ -332,6 +388,9 @@
             pltpu.VMEM((n, rows, channels), f32),
             pltpu.VMEM((lats, channels), bf16),
             pltpu.VMEM((n, lats, width), f32),
+            pltpu.VMEM((at_once, high_side, pitch, channels), f32),
+            pltpu.VMEM((at_once, 3, flat + 2 * pitch, channels), bf16),
+            pltpu.VMEM((at_once * flat, channels), f32),
             pltpu.SemaphoreType.DMA((2, line)),
             pltpu.SemaphoreType.DMA((2, line)),
             pltpu.SemaphoreType.DMA((2, 2 * line)),
@@ -343,7 +402,8 @@
             collective_id=0, has_side_effects=True, vmem_limit_bytes=56 * 1024 * 1024
         ),
     )(
-        tok_norm, lat_own, lat_slice, summary_probes, sharp,
+        picture_feature_maps, filters, picture_token_layer_scaling[None, :],
+        jnp.asarray(pick, bf16), lat_own, lat_slice, summary_probes, sharp,
         asking_projection_tensor, lookup, content, final_projection_tensor,
     )
 

time: 187 us -> 173 us (0.925)
  Pallas kernels: 134 us -> 153 us
  local copies, waits for them, and re-layouts: 28.2 us -> 13.2 us
  matrix products: 10.3 us -> 0 us
  other arithmetic: 10.9 us -> 3.93 us
    pallas_call x1, Pallas kernels: 134 us -> 153 us  [per_device(): pl.pallas_call(functools.partial(mixer, n, heads), out_shape=(jax.ShapeDt...]
    conv_general_dilated x1 -> x0, matrix products: 10.3 us -> none  [per_device(): lax.conv_general_dilated(activated, partitioned_filter_tensor, (1, 1), 'S...]
    add x1 -> x0, local copies, waits for them, and re-layouts: 8.51 us -> none  [per_device(): picture_feature_maps.astype(jnp.float32) + RESIDUAL_SCALE * convolved]
    reshape x1 -> x0, local copies, waits for them, and re-layouts: 7.23 us -> none  [per_device(): summed.reshape(-1, channels)]
    convert_element_type x1 -> x0, other arithmetic: 4.52 us -> none  [per_device(): layer_norm(summed.reshape(-1, channels), picture_token_layer_scaling)]
    reduce_sum x2 -> x1, other arithmetic: 4.19 us -> 1.15 us  [layer_norm(): spread = jnp.mean(center * center, axis=-1, keepdims=True)]
    unnamed x10 -> x4, local copies, waits for them, and re-layouts: 8.84 us -> 9.8 us
where the time goes in v2:
time: 173 us; the launch traced here: 171 us
  Pallas kernels  153 us (88%)
  local copies, waits for them, and re-layouts  13.2 us (8%)
  other arithmetic  3.93 us (2%)
    pallas_call x1, Pallas kernels, per_device(): pl.pallas_call(functools.partial(mixer, n, heads), out_shape=(jax.ShapeDt...  153 us
    unnamed x4, local copies, waits for them, and re-layouts  9.8 us

profile of v2, /device:TPU:0, one launch (start us, length us, event | category | flops | bytes accessed | tf_op | source)
XLA Modules:
  0.0 171.3 jit_solution(8216727243415348205)
XLA Ops:
  0.6 0.7 broadcast_multiply_fusion
  1.3 1.1 convert_reduce_fusion
  2.4 1.2 fusion.2
  3.5 1.3 broadcast_in_dim.4.gain_ref
  4.8 0.1 broadcast_in_dim.10
  4.9 0.7 broadcast_in_dim_reshape.3.sharp_ref
  5.6 1.1 fusion.4
  6.7 0.7 constant_dynamic-slice_fusion.lat_slice_ref
  7.4 0.6 pad.4.lat_own_ref
  8.0 1.9 %copy.14.wo_ref = bf16[1536,96]{1,0:T(8,128)(2,1)} copy(bf16[1536,96]{0,1:T(8,128)(2,1)} %param.19) | data formatting | bytes 589824 | tf_op args[8]
  9.9 4.5 %copy.13.maps_ref = bf16[8,10,10,1536]{3,2,1,0:T(8,128)(2,1)} copy(bf16[8,10,10,1536]{3,0,2,1:T(8,128)(2,1)} %param.11) | data formatting | bytes 4915200 | tf_op args[0]
  14.4 153.4 %shard_map.122 = (f32[64,1536]{1,0:T(8,128)}, bf16[64,1536]{1,0:T(8,128)(2,1)}) custom-call(bf16[8,10,10,1536]{3,2,1,0:T(8,128)(2,1)} %copy.13.maps_ref, bf16[1152,1536]{1,0:T(8,128)(2,1)} %bitcast.1, f32[1,1536]{1,0:T(1,128)} %broadcast_in_dim.4.gain_ref, bf16[208,320]{1,0:T(8,128)(2,1)} %constant.29.clone.pick_ref, bf16[16,1536]{1,0:T(8,128)(2,1)} %pad.4.lat_own_ref, ...), custom_call_target="tpu_custom_call" | custom-call | tf_op jit(solution)/shard_map/pallas_call | solution.py:368
  167.9 1.8 %copy.17 = f32[64,1536]{1,0:T(8,128)} copy(f32[64,1536]{1,0:T(8,128)} %get-tuple-element.4) | data formatting | bytes 786432
  169.6 1.6 copy.18
  (3 shorter events, 0.0 us)

commit v3 on v2

--- a/solution.py
+++ b/solution.py
@@ -47,7 +47,7 @@
     gathered, qpart, qrecv, qall, queries, source, u_high, u_low,
     wsum, part, received, att_all, att_low, cols_all,
     plain, act, summed,
-    z_send, y_send, core_send, w_recv, swap_send, swap_recv,
+    z_send, y_send, x_send, core_send, side_send, w_recv, side_recv, swap_send, swap_recv,
 ):
     channels = sharp_ref.shape[1]
     breadth = channels // heads
@@ -59,6 +59,12 @@
     core = lax.rem(me, 2)
     side = lax.rem(me // 2, 2)
     at = me // 4
+    team = lax.axis_index("groups")
+    odd = lax.rem(team, 2)
+    third = shard // 3
+    piece = pl.ds(pl.multiple_of(odd * third, third), 2 * third)
+    spare = pl.ds(pl.multiple_of(odd * 2 * third, third), third)
+    lacking = pl.ds(pl.multiple_of((1 - odd) * 2 * third, third), third)
     weights = (wk_ref, wv_ref)
 
     def place(a, b, c):
@@ -96,49 +102,88 @@
 
     def along(w, k):
         return remote(
-            weights[w], gathered.at[w, me], z_send.at[w, k], w_recv.at[w, me],
+            weights[w].at[piece], gathered.at[w, me, piece], z_send.at[w, k], w_recv.at[w, me],
             place(lax.rem(at + k, line), side, core),
         )
 
     def across(w, a):
-        owner = place(a, side, core)
+        slab = gathered.at[w, place(a, side, core), piece]
         return remote(
-            gathered.at[w, owner], gathered.at[w, owner], y_send.at[w, a], w_recv.at[w, owner],
+            slab, slab, y_send.at[w, a], w_recv.at[w, place(a, side, core)],
             place(at, 1 - side, core),
         )
 
+    def beside(w, a, b, rows_of):
+        slab = gathered.at[w, place(a, b, core), rows_of]
+        return pltpu.make_async_remote_copy(
+            src_ref=slab, dst_ref=slab, send_sem=x_send.at[w, a * 2 + b],
+            recv_sem=side_recv.at[w, place(a, b, core)],
+            device_id={"groups": team + 1 - 2 * odd, "wide": me},
+            device_id_type=pl.DeviceIdType.MESH,
+        )
+
     def over(w, a, b):
-        owner = place(a, b, core)
+        slab = gathered.at[w, place(a, b, core), piece]
         return remote(
-            gathered.at[w, owner], gathered.at[w, owner], core_send.at[w, a * 2 + b],
-            w_recv.at[w, owner], place(at, side, 1 - core),
-        )
-
-    def arrival(w, owner):
+            slab, slab, core_send.at[w, a * 2 + b], w_recv.at[w, place(a, b, core)],
+            place(at, side, 1 - core),
+        )
+
+    def over_side(w, a, b):
+        slab = gathered.at[w, place(a, b, core), lacking]
+        return remote(
+            slab, slab, side_send.at[w, a * 2 + b], side_recv.at[w, place(a, b, core)],
+            place(at, side, 1 - core),
+        )
+
+    def arrival(w, owner, rows_of, sems):
+        slab = gathered.at[w, owner, rows_of]
         remote(
-            gathered.at[w, owner], gathered.at[w, owner], z_send.at[w, 0], w_recv.at[w, owner],
-            place(at, side, 1 - core),
+            slab, slab, z_send.at[w, 0], sems.at[w, owner], place(at, side, 1 - core)
         ).wait_recv()
 
     def line_step(w, k):
         a = lax.rem(at + line - k, line)
-        arrival(w, place(a, side, core))
+        arrival(w, place(a, side, core), piece, w_recv)
         across(w, a).start()
+        beside(w, a, side, spare).start()
         over(w, a, side).start()
 
     def far_step(w, k):
         a = lax.rem(at + line - k, line)
-        arrival(w, place(a, 1 - side, core))
+        arrival(w, place(a, 1 - side, core), piece, w_recv)
+        beside(w, a, 1 - side, spare).start()
         over(w, a, 1 - side).start()
 
+    def side_step(w, k):
+        a = lax.rem(at + line - k, line)
+
+        @pl.when(k > 0)
+        def _():
+            arrival(w, place(a, side, core), lacking, side_recv)
+            over_side(w, a, side).start()
+
+        arrival(w, place(a, 1 - side, core), lacking, side_recv)
+        over_side(w, a, 1 - side).start()
+
     def core_step(w, k):
-        arrival(w, place(k // 2, lax.rem(k, 2), 1 - core))
+        owner = place(k // 2, lax.rem(k, 2), 1 - core)
+        arrival(w, owner, piece, w_recv)
+        arrival(w, owner, lacking, side_recv)
 
     def finish_sends(w):
         def one(k, carry):
-            across(w, k).wait_send()
-            over(w, k, 0).wait_send()
-            over(w, k, 1).wait_send()
+            a = lax.rem(at + line - k, line)
+            across(w, a).wait_send()
+            over(w, a, 0).wait_send()
+            over(w, a, 1).wait_send()
+            over_side(w, a, 0).wait_send()
+            over_side(w, a, 1).wait_send()
+            beside(w, a, 1 - side, spare).wait_send()
+
+            @pl.when(k > 0)
+            def _():
+                beside(w, a, side, spare).wait_send()
             return carry
         loop(line, lambda k: along(w, k).wait_send())
         lax.fori_loop(0, line, one, 0)
@@ -152,7 +197,10 @@
     barrier = pltpu.get_barrier_semaphore()
     loop(n, lambda k: pl.semaphore_signal(
         barrier, inc=1, device_id={"wide": ring(k)}, device_id_type=pl.DeviceIdType.MESH))
-    pl.semaphore_wait(barrier, n - 1)
+    pl.semaphore_signal(
+        barrier, inc=1, device_id={"groups": team + 1 - 2 * odd, "wide": me},
+        device_id_type=pl.DeviceIdType.MESH)
+    pl.semaphore_wait(barrier, n)
 
     partial = jnp.dot(lat_slice_ref[...], wq_ref[...], preferred_element_type=jnp.float32)
     for j in range(n):
@@ -165,6 +213,7 @@
         loop(line, lambda k: along(w, k).start())
         across(w, at).start()
         over(w, at, side).start()
+        over_side(w, at, side).start()
 
     send_own(0)
     frames, high_side, wide_side = maps_ref.shape[:3]
@@ -230,6 +279,7 @@
     swap_start(1, lambda j: qall.at[me], qall)
 
     each(line, lambda k: far_step(0, k))
+    each(line, lambda k: side_step(0, k))
     swap_wait(1, lambda j: qall.at[me], qall)
     for j in range(n):
         queries[j * rows:(j + 1) * rows] = qall[j]
@@ -271,6 +321,8 @@
             stat_sum = jnp.where(lane == first + i, row_sum[i * lats:(i + 1) * lats], stat_sum)
         if first == 0:
             each(line, lambda k: far_step(1, k))
+        if first == per_block:
+            each(line, lambda k: side_step(1, k))
     each(n // 2, lambda k: core_step(1, k))
 
     wsum[...] = jnp.zeros_like(wsum)
@@ -308,12 +360,13 @@
     for j in range(n):
         wsum[j * rows:(j + 1) * rows] = att_all[j]
     att_low[...] = wsum[...].astype(jnp.bfloat16)
-    cols_all[me] = jnp.dot(att_low[...], wo_ref[...], preferred_element_type=jnp.float32)
+    cols = jnp.dot(att_low[...], wo_ref[...], preferred_element_type=jnp.float32)
+    cols_all[me] = cols.astype(jnp.bfloat16)
     swap_start(4, lambda j: cols_all.at[me], cols_all)
     swap_wait(4, lambda j: cols_all.at[me], cols_all)
     wide = wo_ref.shape[1]
     for j in range(n):
-        attended_ref[:, j * wide:(j + 1) * wide] = cols_all[j]
+        attended_ref[:, j * wide:(j + 1) * wide] = cols_all[j].astype(jnp.float32)
     new_ref[...] = (probes_ref[...].astype(jnp.float32) + attended_ref[...]).astype(jnp.bfloat16)
     finish_sends(0)
     finish_sends(1)
@@ -387,13 +440,16 @@
             pltpu.VMEM((n, rows, channels + 2 * LANES), f32),
             pltpu.VMEM((n, rows, channels), f32),
             pltpu.VMEM((lats, channels), bf16),
-            pltpu.VMEM((n, lats, width), f32),
+            pltpu.VMEM((n, lats, width), bf16),
             pltpu.VMEM((at_once, high_side, pitch, channels), f32),
             pltpu.VMEM((at_once, 3, flat + 2 * pitch, channels), bf16),
             pltpu.VMEM((at_once * flat, channels), f32),
             pltpu.SemaphoreType.DMA((2, line)),
             pltpu.SemaphoreType.DMA((2, line)),
             pltpu.SemaphoreType.DMA((2, 2 * line)),
+            pltpu.SemaphoreType.DMA((2, 2 * line)),
+            pltpu.SemaphoreType.DMA((2, 2 * line)),
+            pltpu.SemaphoreType.DMA((2, n)),
             pltpu.SemaphoreType.DMA((2, n)),
             pltpu.SemaphoreType.DMA((5, n)),
             pltpu.SemaphoreType.DMA((5, n)),

time: 173 us -> 148 us (0.86)
  Pallas kernels: 153 us -> 130 us
    pallas_call x1, Pallas kernels: 153 us -> 130 us  [per_device(): pl.pallas_call(functools.partial(mixer, n, heads), out_shape=(jax.ShapeDt...]
where the time goes in v3:
time: 148 us
  Pallas kernels  130 us (88%)
  local copies, waits for them, and re-layouts  13.2 us (9%)
  other arithmetic  3.93 us (3%)
    pallas_call x1, Pallas kernels, per_device(): pl.pallas_call(functools.partial(mixer, n, heads), out_shape=(jax.ShapeDt...  130 us
    unnamed x4, local copies, waits for them, and re-layouts  9.8 us

profile of v3, /device:TPU:0, one launch (start us, length us, event | category | flops | bytes accessed | tf_op | source)
XLA Modules:
  0.0 147.9 jit_solution(12357679908029646452)
XLA Ops:
  0.6 0.7 broadcast_multiply_fusion
  1.3 1.1 convert_reduce_fusion
  2.4 1.2 fusion.2
  3.5 1.3 broadcast_in_dim.4.gain_ref
  4.8 0.1 broadcast_in_dim.10
  4.9 0.7 broadcast_in_dim_reshape.3.sharp_ref
  5.6 1.1 fusion.4
  6.7 0.7 constant_dynamic-slice_fusion.lat_slice_ref
  7.4 0.6 pad.4.lat_own_ref
  8.0 1.9 %copy.14.wo_ref = bf16[1536,96]{1,0:T(8,128)(2,1)} copy(bf16[1536,96]{0,1:T(8,128)(2,1)} %param.19) | data formatting | bytes 589824 | tf_op args[8]
  9.9 4.5 %copy.13.maps_ref = bf16[8,10,10,1536]{3,2,1,0:T(8,128)(2,1)} copy(bf16[8,10,10,1536]{3,0,2,1:T(8,128)(2,1)} %param.11) | data formatting | bytes 4915200 | tf_op args[0]
  14.4 130.1 %shard_map.122 = (f32[64,1536]{1,0:T(8,128)}, bf16[64,1536]{1,0:T(8,128)(2,1)}) custom-call(bf16[8,10,10,1536]{3,2,1,0:T(8,128)(2,1)} %copy.13.maps_ref, bf16[1152,1536]{1,0:T(8,128)(2,1)} %bitcast.1, f32[1,1536]{1,0:T(1,128)} %broadcast_in_dim.4.gain_ref, bf16[208,320]{1,0:T(8,128)(2,1)} %constant.29.clone.pick_ref, bf16[16,1536]{1,0:T(8,128)(2,1)} %pad.4.lat_own_ref, ...), custom_call_target="tpu_custom_call" | custom-call | tf_op jit(solution)/shard_map/pallas_call | solution.py:421
  144.5 1.8 %copy.17 = f32[64,1536]{1,0:T(8,128)} copy(f32[64,1536]{1,0:T(8,128)} %get-tuple-element.4) | data formatting | bytes 786432
  146.2 1.6 %copy.18 = bf16[64,1536]{1,0:T(8,128)(2,1)} copy(bf16[64,1536]{1,0:T(8,128)(2,1)} %get-tuple-element.5) | data formatting | bytes 393216
  (3 shorter events, 0.0 us)
